TPU v7x, 32 devices: a whole 2x2x4 slice. The times are simulated.
32 devices in a mesh: band: 4 (over y, x), tm: 8 (over z, core).
Axes of the slice: x: 2, y: 2, z: 4, core: 2. Of those that a mesh axis runs over, the one named last changes fastest.
Arguments:
- chebyshev: float32 [32, 3, 32768], P(None, None, ('band', 'tm')), may hold values from -0.9 to 0.9
- crossing: int32 [4, 2, 512], P('band'), may hold values from 0 to 4095, as said below
- counts: int32 [4], P('band'), may hold values from 4096 to 8192, as said below
- route: int32 [4, 32], P('band'), may hold values from 0 to 31, each once within a row
- pairs: int32 [4, 2, 32], P('band'), may hold values from 0 to 31, each once within a row
Outputs:
- closest: float32 [128, 256, 256], P('band', 'tm')
Inputs may be any that keep to these rules, and one draw needn't show every extreme that they name: `crossing`: the 1024 slots of one band are distinct and below 4096, so every band's live slots include them. `counts`: some band is full in every draw. `route`: each row is a permutation of the band's 32 tiles. `pairs`: each row of one owner is a permutation of its 32 received tiles.
All inputs are finite; a program needn't handle non-finite values.
Results may differ from a plain program's by a relative error of at most 0.0003.
Values sent between devices are 32-bit elements; how exact they have to be, the bound alone decides.
A program may use at most 64 MiB of HBM per device.

v0:
```python
import functools

import jax
import jax.numpy as jnp
import numpy as np
from jax import lax
from jax.experimental import pallas as pl
from jax.experimental.pallas import tpu as pltpu
from jax.sharding import PartitionSpec as P

SAMPLES = 64
MESH = pl.DeviceIdType.MESH


def shifted(block, axis, distance):
    devices = range(lax.axis_size(axis))
    route = [(i - distance, i) for i in devices if i - distance in devices]
    return lax.ppermute(block, axis, route)


def basis_table(order_count):
    times = -1.0 + (2.0 * np.arange(SAMPLES) + 1.0) / SAMPLES
    return np.cos(np.arange(order_count)[None, :] * np.arccos(times)[:, None])


def table_parts(order_count):
    rest = basis_table(order_count).astype(np.float32)
    parts = []
    for _ in range(3):
        parts.append(rest.astype(jnp.bfloat16).astype(np.float32))
        rest = rest - parts[-1]
    return parts


def split3(values):
    high = values.astype(jnp.bfloat16)
    rest = values - high.astype(jnp.float32)
    middle = rest.astype(jnp.bfloat16)
    low = (rest - middle.astype(jnp.float32)).astype(jnp.bfloat16)
    return high, middle, low


def join3(product, rows):
    return (product[:rows] + product[rows : 2 * rows]) + product[2 * rows : 3 * rows]


def greet(devices):
    barrier = pltpu.get_barrier_semaphore()
    for device in devices:
        pl.semaphore_signal(barrier, inc=1, device_id=device, device_id_type=MESH)
    pl.semaphore_wait(barrier, len(devices))


def spread(count, position, core, partner, device_of, source_of, out_ref, sems):
    send, recv, hand, take, own = sems
    local = pltpu.make_async_copy(source_of(position), out_ref.at[position, core], own)
    local.start()
    out = []
    for hop in range(1, count):
        peer = (position + hop) % count
        copy = pltpu.make_async_remote_copy(
            src_ref=source_of(peer),
            dst_ref=out_ref.at[position, core],
            send_sem=send.at[hop],
            recv_sem=recv.at[hop],
            device_id=device_of(peer),
            device_id_type=MESH,
        )
        copy.start()
        out.append(copy)
    handed = []
    for hop in range(count):
        origin = (position + count - hop) % count
        if hop:
            out[hop - 1].wait_recv()
        copy = pltpu.make_async_remote_copy(
            src_ref=source_of(position) if hop == 0 else out_ref.at[origin, core],
            dst_ref=out_ref.at[origin, core],
            send_sem=hand.at[hop],
            recv_sem=take.at[hop],
            device_id=partner,
            device_id_type=MESH,
        )
        copy.start()
        handed.append(copy)
    for copy in handed:
        copy.wait()
    for copy in out:
        copy.wait_send()
    local.wait()


def spread_sems(count):
    return [pltpu.SemaphoreType.DMA((count,))] * 4 + [pltpu.SemaphoreType.DMA]


def gather_kernel(count, flat_ref, out_ref, *sems):
    me = lax.axis_index("tm")
    core = me % 2
    partner = {"tm": me + 1 - 2 * core}
    position = me // 2

    def device_of(peer):
        return {"tm": peer * 2 + core}

    greet([device_of((position + hop) % count) for hop in range(1, count)] + [partner])
    spread(count, position, core, partner, device_of, lambda peer: flat_ref, out_ref, sems)


def gather(flat, tm_count):
    count = tm_count // 2
    out = pl.pallas_call(
        functools.partial(gather_kernel, count),
        in_specs=[pl.BlockSpec(memory_space=pl.ANY)],
        out_specs=pl.BlockSpec(memory_space=pl.ANY),
        out_shape=jax.ShapeDtypeStruct((count, 2) + flat.shape, jnp.float32),
        scratch_shapes=spread_sems(count),
        compiler_params=pltpu.CompilerParams(collective_id=0, has_side_effects=True),
        name="gather",
    )(flat)
    return out.reshape((tm_count,) + flat.shape)


def exchange_kernel(count, tiles_ref, flags_ref, out_ref, flags_out_ref, flag_send, flag_recv, flag_own, *sems):
    me = lax.axis_index("tm")
    core = me % 2
    partner = {"tm": me + 1 - 2 * core}
    position = lax.axis_index("band")

    def device_of(peer):
        return {"band": peer}

    greet([device_of((position + hop) % count) for hop in range(1, count)] + [partner])
    own = pltpu.make_async_copy(flags_ref.at[position], flags_out_ref.at[position], flag_own)
    own.start()
    flags = []
    for hop in range(1, count):
        peer = (position + hop) % count
        copy = pltpu.make_async_remote_copy(
            src_ref=flags_ref.at[peer],
            dst_ref=flags_out_ref.at[position],
            send_sem=flag_send.at[hop],
            recv_sem=flag_recv.at[hop],
            device_id=device_of(peer),
            device_id_type=MESH,
        )
        copy.start()
        flags.append(copy)
    spread(
        count, position, core, partner, device_of, lambda peer: tiles_ref.at[peer], out_ref, sems
    )
    for copy in flags:
        copy.wait()
    own.wait()


def exchange(tiles, flags, band_count):
    half, rows, tile_size = tiles.shape
    each = half // band_count
    tiles = tiles.reshape(band_count, each, rows, tile_size)
    flags = flags.reshape(band_count, 2 * each, tile_size)
    out, flags_out = pl.pallas_call(
        functools.partial(exchange_kernel, band_count),
        in_specs=[pl.BlockSpec(memory_space=pl.ANY)] * 2,
        out_specs=[pl.BlockSpec(memory_space=pl.ANY)] * 2,
        out_shape=[
            jax.ShapeDtypeStruct((band_count, 2, each, rows, tile_size), jnp.float32),
            jax.ShapeDtypeStruct(flags.shape, jnp.float32),
        ],
        scratch_shapes=[
            pltpu.SemaphoreType.DMA((band_count,)),
            pltpu.SemaphoreType.DMA((band_count,)),
            pltpu.SemaphoreType.DMA,
        ]
        + spread_sems(band_count),
        compiler_params=pltpu.CompilerParams(collective_id=1, has_side_effects=True),
        name="exchange",
    )(tiles, flags)
    return out.reshape(2 * half, rows, tile_size), flags_out.reshape(2 * half, tile_size)


def pick_kernel(slots_ref, shards_ref, rise_ref, fall_ref):
    steps, rows, width = shards_ref.shape
    ranks = slots_ref.shape[1]
    slot_ids = lax.broadcasted_iota(jnp.int32, (width, ranks), 0)
    total = None
    for step in range(steps):
        hit = slots_ref[...] - step * width == slot_ids
        one_hot = hit.astype(jnp.float32).astype(jnp.bfloat16)
        parts = jnp.concatenate(split3(shards_ref[step]), axis=0)
        product = jnp.dot(parts, one_hot, preferred_element_type=jnp.float32)
        total = product if total is None else total + product
    joined = join3(total, rows)
    rise_ref[...] = joined[:, : ranks // 2]
    fall_ref[...] = joined[:, ranks // 2 :]


def pick(whole, slots_row, steps):
    _, rows, width = whole.shape
    ranks = slots_row.shape[1]
    half = jax.ShapeDtypeStruct((rows, ranks // 2), jnp.float32)
    return pl.pallas_call(
        pick_kernel,
        grid=(1,),
        in_specs=[
            pl.BlockSpec((1, ranks), lambda i: (0, 0)),
            pl.BlockSpec((steps, rows, width), lambda i: (0, 0, 0)),
        ],
        out_specs=[pl.BlockSpec((rows, ranks // 2), lambda i: (0, 0))] * 2,
        out_shape=[half, half],
        compiler_params=pltpu.CompilerParams(vmem_limit_bytes=40 * 2**20),
        name="pick",
    )(slots_row, whole)


def place_kernel(crossing_tiles, route_ref, slots_ref, tile_ref, rise_ref, fall_ref, out_ref, parts):
    step = pl.program_id(0)
    rows, width = tile_ref.shape[1:]
    ranks = slots_ref.shape[0]
    tile_id = route_ref[step]

    @pl.when(step == 0)
    def _():
        joined = jnp.concatenate([rise_ref[...], fall_ref[...]], axis=1)
        parts[...] = jnp.concatenate(split3(joined), axis=0)

    @pl.when(tile_id >= crossing_tiles)
    def _():
        out_ref[...] = tile_ref[...]

    @pl.when(tile_id < crossing_tiles)
    def _():
        slot_ids = lax.broadcasted_iota(jnp.int32, (ranks, width), 1) + tile_id * width
        hit = (slots_ref[...] == slot_ids).astype(jnp.float32)
        one_hot = hit.astype(jnp.bfloat16)
        taken = jnp.sum(hit, axis=0, keepdims=True)
        product = jnp.dot(parts[...], one_hot, preferred_element_type=jnp.float32)
        out_ref[0] = jnp.where(taken > 0.0, join3(product, rows), tile_ref[0])


def place(whole, slots_column, climbers, sinkers, route, tile_size, crossing_tiles):
    _, rows, width = whole.shape
    ranks = slots_column.shape[0]
    tile_count = route.shape[0]
    per_shard = width // tile_size
    return pl.pallas_call(
        functools.partial(place_kernel, crossing_tiles),
        grid_spec=pltpu.PrefetchScalarGridSpec(
            num_scalar_prefetch=1,
            grid=(tile_count,),
            in_specs=[
                pl.BlockSpec((ranks, 1), lambda i, r: (0, 0)),
                pl.BlockSpec(
                    (1, rows, tile_size),
                    lambda i, r: (r[i] // per_shard, 0, r[i] % per_shard),
                ),
                pl.BlockSpec((rows, ranks // 2), lambda i, r: (0, 0)),
                pl.BlockSpec((rows, ranks // 2), lambda i, r: (0, 0)),
            ],
            out_specs=pl.BlockSpec((1, rows, tile_size), lambda i, r: (i, 0, 0)),
            scratch_shapes=[pltpu.VMEM((3 * rows, ranks), jnp.bfloat16)],
        ),
        out_shape=jax.ShapeDtypeStruct((tile_count, rows, tile_size), jnp.float32),
        compiler_params=pltpu.CompilerParams(vmem_limit_bytes=40 * 2**20),
        name="place",
    )(route, slots_column, whole, climbers, sinkers)


def pair_kernel(
    share,
    first_ids,
    second_ids,
    live,
    place_ref,
    tiles_ref,
    alive_ref,
    table_ref,
    table_t_ref,
    out_ref,
    turned,
    first_pos,
    second_pos,
):
    step = pl.program_id(0)
    first_id = first_ids[step]
    second_id = second_ids[step]
    lanes = turned.shape[0]
    both = live[first_id] * live[second_id]

    @pl.when(both == 0)
    def _():
        out_ref[...] = jnp.zeros_like(out_ref)

    @pl.when(both != 0)
    def _():
        columns = pl.ds(pl.multiple_of(place_ref[0] * lanes, lanes), lanes)
        window = tiles_ref[first_id, :, columns]
        rows = window.shape[0]
        flags = jnp.broadcast_to(alive_ref[first_id, :, columns], (8, lanes))
        turned[...] = jnp.concatenate([window, flags], axis=0).T
        mine = turned[pl.ds(pl.multiple_of(place_ref[1], share), share), :]
        parts = jnp.concatenate(split3(mine[:, :rows]), axis=0)
        product = jnp.dot(parts, table_t_ref[...], preferred_element_type=jnp.float32)
        wide = first_pos.shape[1]

        def term(part, table_part):
            return product[part * share : (part + 1) * share, table_part * wide : (table_part + 1) * wide]

        first_pos[...] = term(0, 0) + (
            (term(0, 1) + term(1, 0)) + ((term(1, 1) + term(0, 2)) + term(2, 0))
        )
        high, middle, low = split3(tiles_ref[second_id])
        orders = rows // 3
        for c in range(3):
            mine_rows = slice(c * orders, (c + 1) * orders)
            packed = [part[mine_rows] for part in (high, middle, high, middle, low, high)]
            second_pos[c * SAMPLES : (c + 1) * SAMPLES, :] = jnp.dot(
                table_ref[...],
                jnp.concatenate(packed, axis=0),
                preferred_element_type=jnp.float32,
            )
        closest = None
        for s in range(SAMPLES):
            gaps = [
                first_pos[:, c * SAMPLES + s : c * SAMPLES + s + 1]
                - second_pos[c * SAMPLES + s : c * SAMPLES + s + 1, :]
                for c in range(3)
            ]
            square = (gaps[0] * gaps[0] + gaps[1] * gaps[1]) + gaps[2] * gaps[2]
            closest = square if closest is None else jnp.minimum(closest, square)
        out_ref[0] = closest * (mine[:, rows : rows + 1] * alive_ref[second_id])


def pair_blocks(tiles, alive, first_ids, second_ids, row_start, share):
    tile_count, rows, tile_size = tiles.shape
    orders = rows // 3
    wide = 256
    high, middle, low = table_parts(orders)
    table = np.concatenate([high, high, middle, middle, high, low], axis=1)
    spread_parts = [
        np.pad(np.kron(np.eye(3), part.T), ((0, 0), (0, wide - 3 * SAMPLES)))
        for part in (high, middle, low)
    ]
    table_t = np.concatenate(spread_parts, axis=1)
    table, table_t = (jnp.asarray(t, jnp.bfloat16) for t in (table, table_t))
    live = (jnp.max(alive, axis=1) > 0.0).astype(jnp.int32)
    lanes = min(128, tile_size)
    position = jnp.stack([row_start // lanes, row_start % lanes]).astype(jnp.int32)
    alive = alive.reshape(tile_count, 1, tile_size)
    return pl.pallas_call(
        functools.partial(pair_kernel, share),
        grid_spec=pltpu.PrefetchScalarGridSpec(
            num_scalar_prefetch=4,
            grid=(tile_count,),
            in_specs=[
                pl.BlockSpec(tiles.shape, lambda i, a, b, l, w: (0, 0, 0)),
                pl.BlockSpec(alive.shape, lambda i, a, b, l, w: (0, 0, 0)),
                pl.BlockSpec(table.shape, lambda i, a, b, l, w: (0, 0)),
                pl.BlockSpec(table_t.shape, lambda i, a, b, l, w: (0, 0)),
            ],
            out_specs=pl.BlockSpec((1, share, tile_size), lambda i, a, b, l, w: (i, 0, 0)),
            scratch_shapes=[
                pltpu.VMEM((lanes, rows + 8), jnp.float32),
                pltpu.VMEM((share, wide), jnp.float32),
                pltpu.VMEM((3 * SAMPLES, tile_size), jnp.float32),
            ],
        ),
        out_shape=jax.ShapeDtypeStruct((tile_count, share, tile_size), jnp.float32),
        compiler_params=pltpu.CompilerParams(vmem_limit_bytes=40 * 2**20),
        name="pair_blocks",
    )(first_ids, second_ids, live, position, tiles, alive, table, table_t)


def on_device(chebyshev, crossing, counts, route, pairs):
    orders, _, local = chebyshev.shape
    tm_count = lax.axis_size("tm")
    tile_count = route.shape[1]
    obj_count = local * tm_count
    tile_size = obj_count // tile_count
    share = tile_size // tm_count
    row_start = lax.axis_index("tm") * share

    flat = chebyshev.transpose(1, 0, 2).reshape(3 * orders, local)
    whole = gather(flat, tm_count)

    slot_ids = jnp.arange(tile_size, dtype=jnp.int32)[None, :] + tile_size * route[0][:, None]
    alive_out = (slot_ids < counts[0]).astype(jnp.float32)

    slots_row = crossing[0].reshape(1, -1)
    rising, falling = pick(whole, slots_row, (tm_count + 1) // 2)
    climbers = shifted(rising, "band", 1)
    sinkers = shifted(falling, "band", -1)
    band_count = lax.axis_size("band")
    core = lax.axis_index("tm") % 2
    halves = route[0].reshape(band_count, 2, tile_count // band_count // 2)
    mine = lax.dynamic_index_in_dim(halves, core, 1, keepdims=False).reshape(-1)
    slots_column = crossing[0].reshape(-1, 1)
    outgoing = place(whole, slots_column, climbers, sinkers, mine, tile_size, tile_count // 2)
    tiles, alive = exchange(outgoing, alive_out, band_count)
    return pair_blocks(tiles, alive, pairs[0, 0], pairs[0, 1], row_start, share)


def solution(mesh):
    placed = (
        P(None, None, ("band", "tm")),
        P("band", None, None),
        P("band"),
        P("band", None),
        P("band", None, None),
    )
    return jax.shard_map(
        on_device, mesh=mesh, in_specs=placed, out_specs=P("band", "tm", None), check_vma=False
    )
```

profile of v0, /device:TPU:25, one launch (start us, length us, event | category | flops | bytes accessed | tf_op | source)
XLA Modules:
  0.0 137.3 jit_solution(16307250135206709249)
XLA Ops:
  0.0 0.0 copy-start.7
  0.0 0.0 copy-start.8
  0.0 40.3 %gather.1 = f32[4,2,96,1024]{3,2,1,0:T(8,128)} custom-call(f32[96,1024]{1,0:T(8,128)} %bitcast.26), custom_call_target="tpu_custom_call" | custom-call | tf_op jit(solution)/shard_map/gather/pallas_call | solution.py:112
  40.3 0.0 copy-done.7
  40.3 0.0 copy-start
  40.3 1.9 %copy-done = f32[4,2,96,1024]{3,2,1,0:T(8,128)S(1)} copy-done((f32[4,2,96,1024]{3,2,1,0:T(8,128)S(1)}, f32[4,2,96,1024]{3,2,1,0:T(8,128)}, u32[]{:S(2)}) %copy-start) | copy-done | bytes 3145752
  42.2 0.0 copy-start.1
  42.2 3.4 %pick.1 = (f32[96,512]{1,0:T(8,128)}, f32[96,512]{1,0:T(8,128)}) custom-call(s32[1,1024]{1,0:T(1,128)S(1)} %bitcast.24, f32[8,96,1024]{2,1,0:T(8,128)S(1)} %bitcast.19), custom_call_target="tpu_custom_call" | custom-call | tf_op jit(solution)/shard_map/pick/pallas_call | solution.py:202
  45.6 3.1 %collective-permute-start = (f32[96,512]{1,0:T(8,128)}, f32[96,512]{1,0:T(8,128)S(1)}, u32[]{:S(2)}, u32[]{:S(2)}) collective-permute-start(f32[96,512]{1,0:T(8,128)} %get-tuple-element.9), channel_id=1, source_target_pairs={{0,8},{8,16},{16,24},{1,9},{9,17},{17,25},{2,10},{10,18},{18,26},{... | collective-permute-start | bytes 589832 | tf_op jit(solution)/shard_map/ppermute | solution.py:18
  48.7 1.3 collective-permute-start.1
  50.0 1.0 copy.10
  51.1 0.5 broadcast.27
  51.6 0.0 copy-done.8
  51.6 0.6 multiply_reduce_fusion
  52.2 0.1 reshape_squeeze.9
  52.3 0.1 reshape.40.route_ref
  52.4 0.1 mul.19
  53.2 0.7 fusion.flags_ref
  53.8 0.1 pad_add_fusion.place_ref
  53.9 0.8 slice_bitcast_fusion
  54.7 0.0 collective-permute-done.rise_ref
  54.7 4.5 %collective-permute-done.1.fall_ref = f32[96,512]{1,0:T(8,128)S(1)} collective-permute-done((f32[96,512]{1,0:T(8,128)}, f32[96,512]{1,0:T(8,128)S(1)}, u32[]{:S(2)}, u32[]{:S(2)}) %collective-permute-start.1) | collective-permute-done | bytes 196640 | tf_op jit(solution)/shard_map/ppermute | solution.py:18
  59.2 0.0 copy-done.1
  59.2 0.0 copy-start.4
  59.2 1.0 copy-done.4
  60.3 6.3 %place.1 = f32[16,96,256]{2,1,0:T(8,128)S(1)} custom-call(s32[16]{0:T(128)S(1)} %reshape.40.route_ref, s32[1024,1]{1,0:T(8,128)S(1)} %bitcast.23, f32[8,96,1024]{2,1,0:T(8,128)S(1)} %bitcast.20, f32[96,512]{1,0:T(8,128)S(1)} %collective-permute-done.rise_ref, f32[96,512]{1,0:T(8,128)S(1)} %collective-permute-done.1.fall_ref), custom_call_target="tpu_custom_call" | custom-call | tf_op jit(solution)/shard_map/place/pallas_call | solution.py:246
  66.6 0.0 copy-start.2
  66.6 1.1 copy-done.2
  67.8 23.1 %exchange.1 = (f32[4,2,4,96,256]{4,3,2,1,0:T(8,128)}, f32[4,8,256]{2,1,0:T(8,128)}) custom-call(f32[4,4,96,256]{3,2,1,0:T(8,128)} %bitcast.21, f32[4,8,256]{2,1,0:T(8,128)} %fusion.flags_ref), custom_call_target="tpu_custom_call" | custom-call | tf_op jit(solution)/shard_map/exchange/pallas_call | solution.py:162
  90.8 0.8 reshape_reshape.3.alive_ref
  91.6 0.8 reduce_max.9
  92.5 0.1 reshape.45.live
  92.6 0.0 copy-start.3
  92.6 1.9 %copy-done.3 = f32[4,2,4,96,256]{4,3,2,1,0:T(8,128)S(1)} copy-done((f32[4,2,4,96,256]{4,3,2,1,0:T(8,128)S(1)}, f32[4,2,4,96,256]{4,3,2,1,0:T(8,128)}, u32[]{:S(2)}) %copy-start.3) | copy-done | bytes 3145752
  94.5 0.0 copy-start.5
  94.5 0.9 copy-done.5
  95.4 0.0 copy-start.6
  95.4 0.8 copy-done.6
  96.1 41.1 %pair_blocks.1 = f32[32,32,256]{2,1,0:T(8,128)} custom-call(s32[32]{0:T(128)S(1)} %get-tuple-element.16.first_ids, s32[32]{0:T(128)S(1)} %get-tuple-element.15.second_ids, s32[32]{0:T(128)S(1)} %reshape.45.live, s32[2]{0:T(128)S(1)} %pad_add_fusion.place_ref, f32[32,96,256]{2,1,0:T(8,128)S(1)} %bitcast.22, f32[32,1,256]{2,1,0:T(1,128)S(1)} %reshape_reshape.3.alive_ref, ...), custom_call_target="tpu_custom_call" | custom-call | tf_op jit(solution)/shard_map/pair_blocks/pallas_call | solution.py:350
  (3 shorter events, 0.0 us)
Async XLA Ops:
  0.0 40.3 %copy-start.7 = (s32[1,2,512]{2,1,0:T(2,128)S(1)}, s32[1,2,512]{2,1,0:T(2,128)}, u32[]{:S(2)}) copy-start(s32[1,2,512]{2,1,0:T(2,128)} %param.8) | copy-start | bytes 12292
  0.0 51.6 %copy-start.8 = (s32[1,32]{1,0:T(1,128)S(1)}, s32[1,32]{1,0:T(1,128)}, u32[]{:S(2)}) copy-start(s32[1,32]{1,0:T(1,128)} %param.10) | copy-start | bytes 388
  40.3 1.9 %copy-start = (f32[4,2,96,1024]{3,2,1,0:T(8,128)S(1)}, f32[4,2,96,1024]{3,2,1,0:T(8,128)}, u32[]{:S(2)}) copy-start(f32[4,2,96,1024]{3,2,1,0:T(8,128)} %gather.1) | copy-start | bytes 9437188
  42.2 17.0 %copy-start.1 = (f32[4,2,96,1024]{3,2,1,0:T(8,128)S(1)}, f32[4,2,96,1024]{3,2,1,0:T(8,128)}, u32[]{:S(2)}) copy-start(f32[4,2,96,1024]{3,2,1,0:T(8,128)} %gather.1) | copy-start | bytes 9437188
  45.6 9.1 %collective-permute-start = (f32[96,512]{1,0:T(8,128)}, f32[96,512]{1,0:T(8,128)S(1)}, u32[]{:S(2)}, u32[]{:S(2)}) collective-permute-start(f32[96,512]{1,0:T(8,128)} %get-tuple-element.9), channel_id=1, source_target_pairs={{0,8},{8,16},{16,24},{1,9},{9,17},{17,25},{2,10},{10,18},{18,26},{... | collective-permute-start | bytes 589832 | tf_op jit(solution)/shard_map/ppermute | solution.py:18
  48.7 10.5 %collective-permute-start.1 = (f32[96,512]{1,0:T(8,128)}, f32[96,512]{1,0:T(8,128)S(1)}, u32[]{:S(2)}, u32[]{:S(2)}) collective-permute-start(f32[96,512]{1,0:T(8,128)} %get-tuple-element.10), channel_id=1, source_target_pairs={{8,0},{16,8},{24,16},{9,1},{17,9},{25,17},{10,2},{18,10},{26,18},{... | collective-permute-start | bytes 589832 | tf_op jit(solution)/shard_map/ppermute | solution.py:18
  59.2 1.0 copy-start.4
  66.6 1.2 copy-start.2
  92.6 1.9 %copy-start.3 = (f32[4,2,4,96,256]{4,3,2,1,0:T(8,128)S(1)}, f32[4,2,4,96,256]{4,3,2,1,0:T(8,128)}, u32[]{:S(2)}) copy-start(f32[4,2,4,96,256]{4,3,2,1,0:T(8,128)} %get-tuple-element.12) | copy-start | bytes 9437188
  94.5 0.9 copy-start.5
  95.4 0.8 copy-start.6
where the time goes:
time: 138 us; the launch traced here: 137 us
  Pallas kernels  114 us (83%)
  local copies, waits for them, and re-layouts  11.1 us (8%)
  waiting for transfers between devices  4.53 us (3%)
  starting transfers between devices  4.41 us (3%)
  other arithmetic  2.24 us (2%)
    pallas_call x1, Pallas kernels, pair_blocks(): pl.pallas_call(functools.partial(pair_kernel, share), grid_spec=pltpu.Pre...  41.1 us
    pallas_call x1, Pallas kernels, gather(): pl.pallas_call(functools.partial(gather_kernel, count), in_specs=[pl.Bloc...  40.3 us
    pallas_call x1, Pallas kernels, exchange(): pl.pallas_call(functools.partial(exchange_kernel, band_count), in_specs=[...  23.1 us
    unnamed x21, local copies, waits for them, and re-layouts  9.19 us
    pallas_call x1, Pallas kernels, place(): pl.pallas_call(functools.partial(place_kernel, crossing_tiles), grid_spec...  6.34 us
    ppermute x2, waiting for transfers between devices, shifted(): return lax.ppermute(block, axis, route)  4.53 us
    ppermute x2, starting transfers between devices, shifted(): return lax.ppermute(block, axis, route)  4.41 us
    pallas_call x1, Pallas kernels, pick(): pl.pallas_call(pick_kernel, grid=(1,), in_specs=[pl.BlockSpec((1, ranks),...  3.36 us
  transfers between devices with their start and end apart: 2, of which 1 were waited for; matrix products, arithmetic and copies ran while one was open for 3% of the time, Pallas kernels for 0%

commit v1 on v0

--- a/solution.py
+++ b/solution.py
@@ -51,47 +51,55 @@
     pl.semaphore_wait(barrier, len(devices))
 
 
-def spread(count, position, core, partner, device_of, source_of, out_ref, sems):
+def spread(count, pieces, position, core, partner, device_of, source_of, out_ref, sems):
     send, recv, hand, take, own = sems
     local = pltpu.make_async_copy(source_of(position), out_ref.at[position, core], own)
     local.start()
-    out = []
-    for hop in range(1, count):
-        peer = (position + hop) % count
-        copy = pltpu.make_async_remote_copy(
-            src_ref=source_of(peer),
-            dst_ref=out_ref.at[position, core],
-            send_sem=send.at[hop],
-            recv_sem=recv.at[hop],
-            device_id=device_of(peer),
-            device_id_type=MESH,
-        )
-        copy.start()
-        out.append(copy)
+    size = out_ref.shape[2] // pieces
+    out = {}
+    for piece in range(pieces):
+        cut = pl.ds(piece * size, size)
+        for hop in range(1, count):
+            peer = (position + hop) % count
+            copy = pltpu.make_async_remote_copy(
+                src_ref=source_of(peer).at[cut],
+                dst_ref=out_ref.at[position, core, cut],
+                send_sem=send.at[piece * count + hop],
+                recv_sem=recv.at[piece * count + hop],
+                device_id=device_of(peer),
+                device_id_type=MESH,
+            )
+            copy.start()
+            out[piece, hop] = copy
     handed = []
-    for hop in range(count):
-        origin = (position + count - hop) % count
-        if hop:
-            out[hop - 1].wait_recv()
-        copy = pltpu.make_async_remote_copy(
-            src_ref=source_of(position) if hop == 0 else out_ref.at[origin, core],
-            dst_ref=out_ref.at[origin, core],
-            send_sem=hand.at[hop],
-            recv_sem=take.at[hop],
-            device_id=partner,
-            device_id_type=MESH,
-        )
-        copy.start()
-        handed.append(copy)
+    for piece in range(pieces):
+        cut = pl.ds(piece * size, size)
+        for hop in range(count):
+            origin = (position + count - hop) % count
+            if hop:
+                out[piece, hop].wait_recv()
+                source = out_ref.at[origin, core, cut]
+            else:
+                source = source_of(position).at[cut]
+            copy = pltpu.make_async_remote_copy(
+                src_ref=source,
+                dst_ref=out_ref.at[origin, core, cut],
+                send_sem=hand.at[piece * count + hop],
+                recv_sem=take.at[piece * count + hop],
+                device_id=partner,
+                device_id_type=MESH,
+            )
+            copy.start()
+            handed.append(copy)
     for copy in handed:
         copy.wait()
-    for copy in out:
+    for copy in out.values():
         copy.wait_send()
     local.wait()
 
 
-def spread_sems(count):
-    return [pltpu.SemaphoreType.DMA((count,))] * 4 + [pltpu.SemaphoreType.DMA]
+def spread_sems(count, pieces):
+    return [pltpu.SemaphoreType.DMA((count * pieces,))] * 4 + [pltpu.SemaphoreType.DMA]
 
 
 def gather_kernel(count, flat_ref, out_ref, *sems):
@@ -104,7 +112,7 @@
         return {"tm": peer * 2 + core}
 
     greet([device_of((position + hop) % count) for hop in range(1, count)] + [partner])
-    spread(count, position, core, partner, device_of, lambda peer: flat_ref, out_ref, sems)
+    spread(count, 4, position, core, partner, device_of, lambda peer: flat_ref, out_ref, sems)
 
 
 def gather(flat, tm_count):
@@ -114,7 +122,7 @@
         in_specs=[pl.BlockSpec(memory_space=pl.ANY)],
         out_specs=pl.BlockSpec(memory_space=pl.ANY),
         out_shape=jax.ShapeDtypeStruct((count, 2) + flat.shape, jnp.float32),
-        scratch_shapes=spread_sems(count),
+        scratch_shapes=spread_sems(count, 4),
         compiler_params=pltpu.CompilerParams(collective_id=0, has_side_effects=True),
         name="gather",
     )(flat)
@@ -147,7 +155,15 @@
         copy.start()
         flags.append(copy)
     spread(
-        count, position, core, partner, device_of, lambda peer: tiles_ref.at[peer], out_ref, sems
+        count,
+        min(2, out_ref.shape[2]),
+        position,
+        core,
+        partner,
+        device_of,
+        lambda peer: tiles_ref.at[peer],
+        out_ref,
+        sems,
     )
     for copy in flags:
         copy.wait()
@@ -172,7 +188,7 @@
             pltpu.SemaphoreType.DMA((band_count,)),
             pltpu.SemaphoreType.DMA,
         ]
-        + spread_sems(band_count),
+        + spread_sems(band_count, min(2, each)),
         compiler_params=pltpu.CompilerParams(collective_id=1, has_side_effects=True),
         name="exchange",
     )(tiles, flags)

time: 138 us -> 142 us (1.029); the launches traced: 137 us -> 143 us
  Pallas kernels: 114 us -> 120 us
    pallas_call x1, Pallas kernels: 41.1 us -> 47.8 us  [pair_blocks(): pl.pallas_call(functools.partial(pair_kernel, share), grid_spec=pltpu.Pre...]
    pallas_call x1, Pallas kernels: 6.34 us -> 4.22 us  [place(): pl.pallas_call(functools.partial(place_kernel, crossing_tiles), grid_spec...]
    pallas_call x1, Pallas kernels: 23.1 us -> 24.7 us  [exchange(): pl.pallas_call(functools.partial(exchange_kernel, band_count), in_specs=[...]
where the time goes in v1:
time: 142 us; the launch traced here: 143 us
  Pallas kernels  120 us (85%)
  local copies, waits for them, and re-layouts  11.1 us (8%)
  waiting for transfers between devices  4.52 us (3%)
  starting transfers between devices  4.41 us (3%)
  other arithmetic  2.24 us (2%)
    pallas_call x1, Pallas kernels, pair_blocks(): pl.pallas_call(functools.partial(pair_kernel, share), grid_spec=pltpu.Pre...  47.8 us
    pallas_call x1, Pallas kernels, gather(): pl.pallas_call(functools.partial(gather_kernel, count), in_specs=[pl.Bloc...  39.9 us
    pallas_call x1, Pallas kernels, exchange(): pl.pallas_call(functools.partial(exchange_kernel, band_count), in_specs=[...  24.7 us
    unnamed x21, local copies, waits for them, and re-layouts  9.19 us
    ppermute x2, waiting for transfers between devices, shifted(): return lax.ppermute(block, axis, route)  4.52 us
    ppermute x2, starting transfers between devices, shifted(): return lax.ppermute(block, axis, route)  4.41 us
    pallas_call x1, Pallas kernels, place(): pl.pallas_call(functools.partial(place_kernel, crossing_tiles), grid_spec...  4.22 us
    pallas_call x1, Pallas kernels, pick(): pl.pallas_call(pick_kernel, grid=(1,), in_specs=[pl.BlockSpec((1, ranks),...  3.36 us
  transfers between devices with their start and end apart: 2, of which 1 were waited for; matrix products, arithmetic and copies ran while one was open for 3% of the time, Pallas kernels for 0%

profile of v1, /device:TPU:25, one launch (start us, length us, event | category | flops | bytes accessed | tf_op | source)
XLA Modules:
  0.0 143.1 jit_solution(3505178112601338129)
XLA Ops:
  0.0 0.0 copy-start.7
  0.0 0.0 copy-start.8
  0.0 39.9 %gather.1 = f32[4,2,96,1024]{3,2,1,0:T(8,128)} custom-call(f32[96,1024]{1,0:T(8,128)} %bitcast.26), custom_call_target="tpu_custom_call" | custom-call | tf_op jit(solution)/shard_map/gather/pallas_call | solution.py:120
  39.9 0.0 copy-done.7
  39.9 0.0 copy-start
  39.9 1.9 %copy-done = f32[4,2,96,1024]{3,2,1,0:T(8,128)S(1)} copy-done((f32[4,2,96,1024]{3,2,1,0:T(8,128)S(1)}, f32[4,2,96,1024]{3,2,1,0:T(8,128)}, u32[]{:S(2)}) %copy-start) | copy-done | bytes 3145752
  41.8 0.0 copy-start.1
  41.8 3.4 %pick.1 = (f32[96,512]{1,0:T(8,128)}, f32[96,512]{1,0:T(8,128)}) custom-call(s32[1,1024]{1,0:T(1,128)S(1)} %bitcast.24, f32[8,96,1024]{2,1,0:T(8,128)S(1)} %bitcast.19), custom_call_target="tpu_custom_call" | custom-call | tf_op jit(solution)/shard_map/pick/pallas_call | solution.py:218
  45.2 3.1 %collective-permute-start = (f32[96,512]{1,0:T(8,128)}, f32[96,512]{1,0:T(8,128)S(1)}, u32[]{:S(2)}, u32[]{:S(2)}) collective-permute-start(f32[96,512]{1,0:T(8,128)} %get-tuple-element.9), channel_id=1, source_target_pairs={{0,8},{8,16},{16,24},{1,9},{9,17},{17,25},{2,10},{10,18},{18,26},{... | collective-permute-start | bytes 589832 | tf_op jit(solution)/shard_map/ppermute | solution.py:18
  48.3 1.3 collective-permute-start.1
  49.6 1.0 copy.10
  50.7 0.5 broadcast.27
  51.2 0.0 copy-done.8
  51.2 0.6 multiply_reduce_fusion
  51.8 0.1 reshape_squeeze.9
  51.9 0.1 reshape.40.route_ref
  52.0 0.1 mul.19
  52.8 0.7 fusion.flags_ref
  53.5 0.1 pad_add_fusion.place_ref
  53.5 0.8 slice_bitcast_fusion
  54.3 0.0 collective-permute-done.rise_ref
  54.3 4.5 %collective-permute-done.1.fall_ref = f32[96,512]{1,0:T(8,128)S(1)} collective-permute-done((f32[96,512]{1,0:T(8,128)}, f32[96,512]{1,0:T(8,128)S(1)}, u32[]{:S(2)}, u32[]{:S(2)}) %collective-permute-start.1) | collective-permute-done | bytes 196640 | tf_op jit(solution)/shard_map/ppermute | solution.py:18
  58.8 0.0 copy-done.1
  58.8 0.0 copy-start.4
  58.8 1.0 copy-done.4
  59.9 4.2 %place.1 = f32[16,96,256]{2,1,0:T(8,128)S(1)} custom-call(s32[16]{0:T(128)S(1)} %reshape.40.route_ref, s32[1024,1]{1,0:T(8,128)S(1)} %bitcast.23, f32[8,96,1024]{2,1,0:T(8,128)S(1)} %bitcast.20, f32[96,512]{1,0:T(8,128)S(1)} %collective-permute-done.rise_ref, f32[96,512]{1,0:T(8,128)S(1)} %collective-permute-done.1.fall_ref), custom_call_target="tpu_custom_call" | custom-call | tf_op jit(solution)/shard_map/place/pallas_call | solution.py:262
  64.1 0.0 copy-start.2
  64.1 1.1 copy-done.2
  65.2 24.7 %exchange.1 = (f32[4,2,4,96,256]{4,3,2,1,0:T(8,128)}, f32[4,8,256]{2,1,0:T(8,128)}) custom-call(f32[4,4,96,256]{3,2,1,0:T(8,128)} %bitcast.21, f32[4,8,256]{2,1,0:T(8,128)} %fusion.flags_ref), custom_call_target="tpu_custom_call" | custom-call | tf_op jit(solution)/shard_map/exchange/pallas_call | solution.py:178
  90.0 0.8 reshape_reshape.3.alive_ref
  90.8 0.8 reduce_max.9
  91.6 0.1 reshape.45.live
  91.7 0.0 copy-start.3
  91.7 1.9 %copy-done.3 = f32[4,2,4,96,256]{4,3,2,1,0:T(8,128)S(1)} copy-done((f32[4,2,4,96,256]{4,3,2,1,0:T(8,128)S(1)}, f32[4,2,4,96,256]{4,3,2,1,0:T(8,128)}, u32[]{:S(2)}) %copy-start.3) | copy-done | bytes 3145752
  93.6 0.0 copy-start.5
  93.6 0.9 copy-done.5
  94.5 0.0 copy-start.6
  94.5 0.8 copy-done.6
  95.3 47.8 %pair_blocks.1 = f32[32,32,256]{2,1,0:T(8,128)} custom-call(s32[32]{0:T(128)S(1)} %get-tuple-element.16.first_ids, s32[32]{0:T(128)S(1)} %get-tuple-element.15.second_ids, s32[32]{0:T(128)S(1)} %reshape.45.live, s32[2]{0:T(128)S(1)} %pad_add_fusion.place_ref, f32[32,96,256]{2,1,0:T(8,128)S(1)} %bitcast.22, f32[32,1,256]{2,1,0:T(1,128)S(1)} %reshape_reshape.3.alive_ref, ...), custom_call_target="tpu_custom_call" | custom-call | tf_op jit(solution)/shard_map/pair_blocks/pallas_call | solution.py:366
  (3 shorter events, 0.0 us)
Async XLA Ops:
  0.0 39.9 %copy-start.7 = (s32[1,2,512]{2,1,0:T(2,128)S(1)}, s32[1,2,512]{2,1,0:T(2,128)}, u32[]{:S(2)}) copy-start(s32[1,2,512]{2,1,0:T(2,128)} %param.8) | copy-start | bytes 12292
  0.0 51.2 %copy-start.8 = (s32[1,32]{1,0:T(1,128)S(1)}, s32[1,32]{1,0:T(1,128)}, u32[]{:S(2)}) copy-start(s32[1,32]{1,0:T(1,128)} %param.10) | copy-start | bytes 388
  39.9 1.9 %copy-start = (f32[4,2,96,1024]{3,2,1,0:T(8,128)S(1)}, f32[4,2,96,1024]{3,2,1,0:T(8,128)}, u32[]{:S(2)}) copy-start(f32[4,2,96,1024]{3,2,1,0:T(8,128)} %gather.1) | copy-start | bytes 9437188
  41.8 17.0 %copy-start.1 = (f32[4,2,96,1024]{3,2,1,0:T(8,128)S(1)}, f32[4,2,96,1024]{3,2,1,0:T(8,128)}, u32[]{:S(2)}) copy-start(f32[4,2,96,1024]{3,2,1,0:T(8,128)} %gather.1) | copy-start | bytes 9437188
  45.2 9.1 %collective-permute-start = (f32[96,512]{1,0:T(8,128)}, f32[96,512]{1,0:T(8,128)S(1)}, u32[]{:S(2)}, u32[]{:S(2)}) collective-permute-start(f32[96,512]{1,0:T(8,128)} %get-tuple-element.9), channel_id=1, source_target_pairs={{0,8},{8,16},{16,24},{1,9},{9,17},{17,25},{2,10},{10,18},{18,26},{... | collective-permute-start | bytes 589832 | tf_op jit(solution)/shard_map/ppermute | solution.py:18
  48.3 10.5 %collective-permute-start.1 = (f32[96,512]{1,0:T(8,128)}, f32[96,512]{1,0:T(8,128)S(1)}, u32[]{:S(2)}, u32[]{:S(2)}) collective-permute-start(f32[96,512]{1,0:T(8,128)} %get-tuple-element.10), channel_id=1, source_target_pairs={{8,0},{16,8},{24,16},{9,1},{17,9},{25,17},{10,2},{18,10},{26,18},{... | collective-permute-start | bytes 589832 | tf_op jit(solution)/shard_map/ppermute | solution.py:18
  58.8 1.0 copy-start.4
  64.1 1.2 copy-start.2
  91.7 1.9 %copy-start.3 = (f32[4,2,4,96,256]{4,3,2,1,0:T(8,128)S(1)}, f32[4,2,4,96,256]{4,3,2,1,0:T(8,128)}, u32[]{:S(2)}) copy-start(f32[4,2,4,96,256]{4,3,2,1,0:T(8,128)} %get-tuple-element.12) | copy-start | bytes 9437188
  93.6 0.9 copy-start.5
  94.5 0.8 copy-start.6
